TPU v7x, 128 devices: a whole 4x4x4 slice. The times are simulated.
128 devices in a mesh: seq: 8 (over z_hi, x), tp: 16 (over y, z_lo, core).
Axes of the slice: x: 4, y: 4, z: 4 (z_hi: 2, z_lo: 2; z = z_hi * 2 + z_lo), core: 2. Of those that a mesh axis runs over, the one named last changes fastest.
Arguments:
- activations: bfloat16 [2048, 8192], P('seq', 'tp'), may hold values from -36 to 36
- norm_gain: bfloat16 [8192], P('tp'), may hold values from 0.099609375 to 1.8984375
- in_proj: bfloat16 [8192, 3, 4096], P(None, None, 'tp'), may hold values from -0.0625 to 0.0625
- short_taps: float32 [3, 3, 4096], P(None, None, 'tp'), may hold values from -3.5 to 3.5
- medium_taps: float32 [256, 128], P('tp'), may hold values from -0.5 to 0.5
- cotangent: bfloat16 [2048, 4096], P('seq', 'tp'), may hold values from -1.1953125 to 1.1953125
Outputs:
- mixer_out: bfloat16 [2048, 4096], P('seq', 'tp')
- grad_input: bfloat16 [2048, 8192], P('seq', 'tp')
- grad_proj: bfloat16 [8192, 3, 4096], P('seq', None, 'tp')
All inputs are finite; a program needn't handle non-finite values.
Results may differ from a plain program's by a relative error of at most 0.02.
Values may be sent and summed in bfloat16 or wider, within the bound.
A program may use at most 192 MiB of HBM per device.

v0:
```python
import jax
import jax.numpy as jnp
from jax import lax
from jax.sharding import PartitionSpec as P

GROUP = 16
LS = 3
LM = 128
norm_eps = 1e-06


def shifted(block, axis, distance):
    devices = range(lax.axis_size(axis))
    route = [(i - distance, i) for i in devices if i - distance in devices]
    return lax.ppermute(block, axis, route)


def forward_short(source, taps, offset, length):
    total = jnp.zeros((length,) + source.shape[1:], jnp.float32)
    for index in range(LS):
        total = total + taps[index] * source[offset - index : offset - index + length].astype(
            jnp.float32
        )
    return total


def backward_short(source, taps, length):
    total = jnp.zeros((length,) + source.shape[1:], jnp.float32)
    for index in range(LS):
        total = total + taps[index] * source[index : index + length].astype(jnp.float32)
    return total


def band_matrix(tap_rows, out_len, in_len, lead, sign):
    offsets = lead + sign * (
        lax.broadcasted_iota(jnp.int32, (out_len, in_len), 0)
        - lax.broadcasted_iota(jnp.int32, (out_len, in_len), 1)
    )
    inside = (offsets >= 0) & (offsets < LM)
    picked = jnp.take(tap_rows, jnp.clip(offsets, 0, LM - 1), axis=1)
    return jnp.where(inside[None], picked, 0.0)


def grouped_apply(band, source):
    groups_here = band.shape[0]
    shaped = source.astype(jnp.float32).reshape(source.shape[0], groups_here, GROUP)
    result = jnp.einsum("gts,sgc->tgc", band, shaped, precision=lax.Precision.HIGHEST)
    return result.reshape(band.shape[1], groups_here * GROUP)


def per_device(activations, norm_gain, in_proj, short_taps, medium_taps, cotangent):
    act_full, gain_full = (
        lax.all_gather(activations, "tp", axis=1, tiled=True),
        lax.all_gather(norm_gain, "tp", axis=0, tiled=True),
    )
    tok_rows = act_full.shape[0]
    width = act_full.shape[1]
    local_ch = in_proj.shape[2]
    edge_rows = LM + LS - 2
    head_rows = LS - 1
    act_float = act_full.astype(jnp.float32)
    inv_rms = lax.rsqrt(jnp.mean(act_float * act_float, axis=1, keepdims=True) + norm_eps)
    gain_float = gain_full.astype(jnp.float32)
    normed = (act_float * inv_rms * gain_float).astype(jnp.bfloat16)
    weight = in_proj.reshape(width, 3 * local_ch)
    projected = (
        jnp.dot(normed, weight, preferred_element_type=jnp.float32)
        .astype(jnp.bfloat16)
        .reshape(tok_rows, 3, local_ch)
    )
    kv_tail = projected[tok_rows - edge_rows :, 1:, :].reshape(edge_rows, 2 * local_ch)
    q_tail = projected[tok_rows - head_rows :, 0, :].reshape(head_rows // 2, 2 * local_ch)
    received = shifted(jnp.concatenate([kv_tail, q_tail], 0), "seq", 1)
    kv_ext = jnp.concatenate(
        [received[:edge_rows].reshape(edge_rows, 2, local_ch), projected[:, 1:, :]], 0
    )
    q_ext = jnp.concatenate(
        [received[edge_rows:].reshape(head_rows, local_ch), projected[:, 0, :]], 0
    )
    span = tok_rows + LM - 1
    kv_feat = forward_short(kv_ext, short_taps[:, 1:, :], head_rows, span).astype(jnp.bfloat16)
    q_feat = forward_short(q_ext, short_taps[:, 0, :], head_rows, tok_rows).astype(jnp.bfloat16)
    gated = (kv_feat[:, 0].astype(jnp.float32) * kv_feat[:, 1].astype(jnp.float32)).astype(
        jnp.bfloat16
    )
    band_forward = band_matrix(medium_taps, tok_rows, span, LM - 1, 1)
    filtered = grouped_apply(band_forward, gated)
    mixer_out = (q_feat.astype(jnp.float32) * filtered).astype(jnp.bfloat16)
    grad_out = cotangent.astype(jnp.float32)
    grad_filtered = (grad_out * q_feat.astype(jnp.float32)).astype(jnp.bfloat16)
    grad_q = (grad_out * filtered).astype(jnp.bfloat16)
    kv_own = kv_feat[LM - 1 :]
    front = jnp.concatenate([grad_q[:head_rows, None, :], kv_own[:head_rows]], 1)
    outgoing = jnp.concatenate(
        [grad_filtered[:edge_rows], front.reshape(3 * head_rows, local_ch)], 0
    )
    returned = shifted(outgoing, "seq", -1)
    filt_ext = jnp.concatenate([grad_filtered, returned[:edge_rows]], 0)
    front_next = returned[edge_rows:].reshape(head_rows, 3, local_ch)
    reach = tok_rows + head_rows
    band_backward = band_matrix(medium_taps, reach, tok_rows + edge_rows, 0, -1)
    grad_gated = grouped_apply(band_backward, filt_ext)
    kv_reach = jnp.concatenate([kv_own, front_next[:, 1:, :]], 0)
    q_reach = jnp.concatenate([grad_q, front_next[:, 0, :]], 0)
    grad_k = (grad_gated * kv_reach[:, 1].astype(jnp.float32)).astype(jnp.bfloat16)
    grad_v = (grad_gated * kv_reach[:, 0].astype(jnp.float32)).astype(jnp.bfloat16)
    grad_feat = jnp.stack([q_reach, grad_k, grad_v], 1)
    grad_pre = (
        backward_short(grad_feat, short_taps, tok_rows)
        .astype(jnp.bfloat16)
        .reshape(tok_rows, 3 * local_ch)
    )
    partial_grad = lax.dot_general(
        grad_pre, weight, (((1,), (1,)), ((), ())), preferred_element_type=jnp.float32
    )
    tp_count = lax.axis_size("tp")
    own_width = width // tp_count
    own_scaled = activations.astype(jnp.float32) * inv_rms
    own_gain = norm_gain.astype(jnp.float32)
    whole_grad = lax.psum(partial_grad.astype(jnp.bfloat16), "tp").astype(jnp.float32)
    stat = jnp.mean(gain_float * whole_grad * act_float, axis=1, keepdims=True) * inv_rms
    grad_slice = lax.dynamic_slice_in_dim(
        whole_grad, lax.axis_index("tp") * own_width, own_width, 1
    )
    grad_scaled = own_gain * grad_slice
    grad_input = (inv_rms * (grad_scaled - own_scaled * stat)).astype(jnp.bfloat16)
    row_share = width // lax.axis_size("seq")
    product = lax.dot_general(
        normed, grad_pre, (((0,), (0,)), ((), ())), preferred_element_type=jnp.float32
    )
    grad_proj = lax.psum_scatter(
        product.reshape(lax.axis_size("seq") * row_share, 3, local_ch).astype(jnp.bfloat16),
        "seq",
        scatter_dimension=0,
        tiled=True,
    )
    return (mixer_out, grad_input, grad_proj)


def solution(mesh):
    return jax.shard_map(
        per_device,
        mesh=mesh,
        in_specs=(
            P("seq", "tp"),
            P("tp"),
            P(None, None, "tp"),
            P(None, None, "tp"),
            P("tp", None),
            P("seq", "tp"),
        ),
        out_specs=(P("seq", "tp"), P("seq", "tp"), P("seq", None, "tp")),
        check_vma=False,
    )
```

profile of v0, /device:TPU:1, one launch (start us, length us, event | category | flops | bytes accessed | tf_op | source)
XLA Modules:
  0.0 847.9 jit_solution(10637052879910510053)
XLA Ops:
  8.6 21.9 %all-gather = bf16[16,1,512]{2,1,0:T(2,128)(2,1)S(1)} all-gather(bf16[1,1,512]{2,1,0:T(2,128)(2,1)S(1)} %reshape.189), channel_id=1, replica_groups=mesh['seq'=8,'tp'=16] {'tp'}, dimensions={0}, use_global_device_ids=true | all-gather | bytes 17408 | tf_op jit(solution)/shard_map/all_gather | solution.py:54
  30.5 16.7 %copy.82 = bf16[8192,3,256]{0,2,1:T(8,128)(2,1)} copy(bf16[8192,3,256]{2,0,1:T(8,128)(2,1)} %param.8) | data formatting | bytes 25165824 | tf_op args[2]
  48.0 179.6 %gather_fusion = f32[98048,16]{1,0:T(8,128)} fusion(f32[16,128]{0,1:T(8,128)S(1)} %copy.88, s32[98304]{0:T(1024)S(1)} %pad_clamp_fusion.1), kind=kCustom, calls=%fused_computation | custom fusion | bytes 12942336 | tf_op jit(solution)/shard_map/jit(_take)/gather | solution.py:40
  227.6 27.7 %copy.89 = f32[98048,16]{0,1:T(8,128)} copy(f32[98048,16]{1,0:T(8,128)} %gather_fusion) | data formatting | bytes 12550144 | tf_op jit(solution)/shard_map/jit(_take)/gather | solution.py:40
  255.3 10.9 %reshape.176 = f32[256,383,16]{1,0,2:T(8,128)} reshape(f32[98048,16]{0,1:T(8,128)} %copy.89) | data formatting | bytes 12550144 | tf_op jit(solution)/shard_map/jit(_take)/gather | solution.py:40
  267.0 182.5 %gather_fusion.1 = f32[99330,16]{1,0:T(8,128)} fusion(f32[16,128]{0,1:T(8,128)S(1)} %copy.88, s32[100352]{0:T(1024)S(1)} %pad_clamp_fusion), kind=kCustom, calls=%fused_computation.1 | custom fusion | bytes 13111560 | tf_op jit(solution)/shard_map/jit(_take)/gather | solution.py:40
  449.5 28.0 %copy.96 = f32[99330,16]{0,1:T(8,128)} copy(f32[99330,16]{1,0:T(8,128)} %gather_fusion.1) | data formatting | bytes 12714240 | tf_op jit(solution)/shard_map/jit(_take)/gather | solution.py:40
  477.5 15.4 %reshape.184 = f32[258,385,16]{1,0,2:T(8,128)} reshape(f32[99330,16]{0,1:T(8,128)} %copy.96) | data formatting | bytes 12714240 | tf_op jit(solution)/shard_map/jit(_take)/gather | solution.py:40
  493.2 3.1 fusion.5
  496.3 9.4 %convolution_convert_fusion.1 = bf16[256,768]{1,0:T(8,128)(2,1)S(1)} fusion(bf16[8192,768]{0,1:T(8,128)(2,1)} %bitcast.82, bf16[256,8192]{1,0:T(8,128)(2,1)} %all-gather.3.cloned.1.call-done, f32[8192]{0:T(1024)S(1)} %bitcast.95, f32[256]{0:T(256)S(1)} %add_rsqrt_fusion), kind=kOutput, calls=%fused_computation.31 | convolution fusion | flops 3229810688 | bytes 17204224 | tf_op jit(solution)/shard_map/dot_general | solution.py:67
  506.4 3.1 collective-permute-start
  509.6 2.8 collective-permute-done
  513.6 6.4 fusion.9
  520.9 1.3 collective-permute-start.1
  522.7 5.1 collective-permute-done.1
  528.5 8.0 fusion.1
  537.3 14.4 %fusion = bf16[256,8192]{1,0:T(8,128)(2,1)} fusion(bf16[256,3,256]{0,2,1:T(8,128)(2,1)S(1)} %add_convert_fusion, bf16[8192,3,256]{2,0,1:T(8,128)(2,1)} %param.8), kind=kOutput, calls=%fused_computation.7 | convolution fusion | flops 3223322624 | bytes 17170432 | tf_op jit(solution)/shard_map/dot_general | solution.py:113
  552.0 10.4 %convolution_convert_fusion = bf16[8192,3,256]{2,0,1:T(8,128)(2,1)} fusion(bf16[256,8192]{1,0:T(8,128)(2,1)} %all-gather.3.cloned.1.call-done, f32[8192]{0:T(1024)S(1)} %bitcast.96, f32[256]{0:T(256)S(1)} %add_rsqrt_fusion, bf16[256,3,256]{0,2,1:T(8,128)(2,1)S(1)} %add_convert_fusion), kind=kOutput, calls=%fused_computation.2 | convolution fusion | flops 3235905536 | bytes 17204224 | tf_op jit(solution)/shard_map/dot_general | solution.py:128
  563.9 120.6 %all-reduce.2.cloned.1.call-done = bf16[256,8192]{1,0:T(8,128)(2,1)} async-done(((bf16[256,8192]{1,0:T(8,128)(2,1)}), bf16[256,8192]{1,0:T(8,128)(2,1)}) %all-reduce.2.cloned.1.call-update) | async-done | bytes 4194320 | tf_op jit(solution)/shard_map/psum | solution.py:120
  684.5 3.3 convert_element_type.148
  687.9 1.3 copy-done.1
  689.2 1.7 fusion.8
  690.9 0.9 multiply_convert_fusion
  691.8 149.6 %reduce-scatter.2.cloned.1.call-done = bf16[1024,3,256]{2,0,1:T(8,128)(2,1)} async-done(((bf16[8192,3,256]{2,0,1:T(8,128)(2,1)}), bf16[1024,3,256]{2,0,1:T(8,128)(2,1)}) %reduce-scatter.2.cloned.1.call-update) | async-done | bytes 1572880 | tf_op jit(solution)/shard_map/reduce_scatter | solution.py:131
  (76 shorter events, 9.7 us)
Async XLA Ops:
  7.2 486.0 %all-gather.3.cloned.1.call-start = ((), (), s32[]{:S(2)}) async-start(), calls=%async_computation.1 | async-start | bytes 4456448 | tf_op jit(solution)/shard_map/all_gather | solution.py:53
  7.9 676.6 %all-reduce.2.cloned.1.call-start = ((), (), s32[]{:S(2)}) async-start(), calls=%async_computation.2 | async-start | bytes 8388608 | tf_op jit(solution)/shard_map/psum | solution.py:120
  30.5 16.8 %copy-start.5 = (f32[16,128]{1,0:T(8,128)S(1)}, f32[16,128]{1,0:T(8,128)}, u32[]{:S(2)}) copy-start(f32[16,128]{1,0:T(8,128)} %param.10) | copy-start | bytes 24580
  255.3 10.9 %copy-start.3 = (bf16[256,256]{1,0:T(8,128)(2,1)S(1)}, bf16[256,256]{1,0:T(8,128)(2,1)}, u32[]{:S(2)}) copy-start(bf16[256,256]{1,0:T(8,128)(2,1)} %param.11) | copy-start | bytes 393220
  477.5 15.6 %copy-start.4 = (f32[3,3,256]{2,1,0:T(4,128)S(1)}, f32[3,3,256]{2,1,0:T(4,128)}, u32[]{:S(2)}) copy-start(f32[3,3,256]{2,1,0:T(4,128)} %param.9) | copy-start | bytes 27652
  506.4 6.0 collective-permute-start
  520.9 6.9 collective-permute-start.1
  551.7 289.7 %reduce-scatter.2.cloned.1.call-start = ((), (), s32[]{:S(2)}) async-start(), calls=%async_computation.3 | async-start | bytes 14155776 | tf_op jit(solution)/shard_map/reduce_scatter | solution.py:131
  562.4 0.7 copy-start.6
  563.9 127.0 %copy-start.2 = (bf16[256,512]{1,0:T(8,128)(2,1)S(1)}, bf16[256,512]{1,0:T(8,128)(2,1)}, u32[]{:S(2)}) copy-start(bf16[256,512]{1,0:T(8,128)(2,1)} %param.6) | copy-start | bytes 786436
  684.5 3.4 copy-start
  684.5 4.7 copy-start.1
Sparse Core Ops, SparseCore 0:
  9.7 40.9 all-gather.2
  551.8 132.6 all-reduce.1
  689.0 152.3 reduce-scatter.1
where the time goes:
time: 849 us; the launch traced here: 848 us
  local copies, waits for them, and re-layouts  468 us (55%)
  waiting for transfers between devices  279 us (33%)
  matrix products  48.6 us (6%)
  blocking collectives  21.9 us (3%)
  between operations  14.1 us (2%)
  other arithmetic  12.1 us (1%)
    gather x6, local copies, waits for them, and re-layouts, band_matrix(): picked = jnp.take(tap_rows, jnp.clip(offsets, 0, LM - 1), axis=1)  444 us
    reduce_scatter x1, waiting for transfers between devices, per_device(): lax.psum_scatter(product.reshape(lax.axis_size('seq') * row_share, 3, loc...  150 us
    psum x1, waiting for transfers between devices, per_device(): lax.psum(partial_grad.astype(jnp.bfloat16), 'tp').astype(jnp.float32)  121 us
    all_gather x1, blocking collectives, per_device(): lax.all_gather(norm_gain, 'tp', axis=0, tiled=True)  21.9 us
    unnamed x22, local copies, waits for them, and re-layouts  20.8 us
  transfers between devices with their start and end apart: 5, of which 4 were waited for; matrix products, arithmetic and copies ran while one was open for 57% of the time, Pallas kernels for 0%

commit v1 on v0

--- a/solution.py
+++ b/solution.py
@@ -117,7 +117,10 @@
     own_width = width // tp_count
     own_scaled = activations.astype(jnp.float32) * inv_rms
     own_gain = norm_gain.astype(jnp.float32)
-    whole_grad = lax.psum(partial_grad.astype(jnp.bfloat16), "tp").astype(jnp.float32)
+    fit_face_now = lambda field, comm_axis: jnp.sum(
+        lax.all_gather(field, axis_name=comm_axis), axis=0
+    )
+    whole_grad = fit_face_now(partial_grad.astype(jnp.bfloat16), "tp").astype(jnp.float32)
     stat = jnp.mean(gain_float * whole_grad * act_float, axis=1, keepdims=True) * inv_rms
     grad_slice = lax.dynamic_slice_in_dim(
         whole_grad, lax.axis_index("tp") * own_width, own_width, 1

time: 849 us -> 1050 us (1.24)
  waiting for transfers between devices: 279 us -> 453 us
  other arithmetic: 12.1 us -> 37.1 us
    all_gather x0 -> x1, waiting for transfers between devices: none -> 321 us  [per_device(): lax.all_gather(field, axis_name=comm_axis)]
    psum x1 -> x0, waiting for transfers between devices: 121 us -> none  [per_device(): lax.psum(partial_grad.astype(jnp.bfloat16), 'tp').astype(jnp.float32)]
    reduce_scatter x1, waiting for transfers between devices: 150 us -> 124 us  [per_device(): lax.psum_scatter(product.reshape(lax.axis_size('seq') * row_share, 3, loc...]
    reduce_sum x0 -> x1, other arithmetic: none -> 25 us  [per_device(): jnp.sum(lax.all_gather(field, axis_name=comm_axis), axis=0)]
  transfers between devices with their start and end apart: 5 -> 5, of which waited for: 4 -> 4; matrix products, arithmetic and copies ran while one was open for 57% -> 48% of each run, Pallas kernels for 0% -> 0%
where the time goes in v1:
time: 1050 us
  local copies, waits for them, and re-layouts  469 us (45%)
  waiting for transfers between devices  453 us (43%)
  matrix products  48.7 us (5%)
  other arithmetic  37.1 us (4%)
  blocking collectives  21.9 us (2%)
  between operations  14.1 us (1%)
    gather x6, local copies, waits for them, and re-layouts, band_matrix(): picked = jnp.take(tap_rows, jnp.clip(offsets, 0, LM - 1), axis=1)  446 us
    all_gather x1, waiting for transfers between devices, per_device(): lax.all_gather(field, axis_name=comm_axis)  321 us
    reduce_scatter x1, waiting for transfers between devices, per_device(): lax.psum_scatter(product.reshape(lax.axis_size('seq') * row_share, 3, loc...  124 us
    reduce_sum x1, other arithmetic, per_device(): jnp.sum(lax.all_gather(field, axis_name=comm_axis), axis=0)  25 us
    all_gather x1, blocking collectives, per_device(): lax.all_gather(norm_gain, 'tp', axis=0, tiled=True)  21.9 us
  transfers between devices with their start and end apart: 5, of which 4 were waited for; matrix products, arithmetic and copies ran while one was open for 48% of the time, Pallas kernels for 0%

profile of v1, /device:TPU:1, one launch (start us, length us, event | category | flops | bytes accessed | tf_op | source)
XLA Modules:
  0.0 1047.8 jit_solution(448735685374157030)
XLA Ops:
  9.0 16.7 %copy.82 = bf16[8192,3,256]{0,2,1:T(8,128)(2,1)} copy(bf16[8192,3,256]{2,0,1:T(8,128)(2,1)} %param.8) | data formatting | bytes 25165824 | tf_op args[2]
  25.7 21.9 %all-gather.1 = bf16[16,1,512]{2,1,0:T(2,128)(2,1)S(1)} all-gather(bf16[1,1,512]{2,1,0:T(2,128)(2,1)S(1)} %reshape.190), channel_id=1, replica_groups=mesh['seq'=8,'tp'=16] {'tp'}, dimensions={0}, use_global_device_ids=true | all-gather | bytes 17408 | tf_op jit(solution)/shard_map/all_gather | solution.py:54
  48.3 180.4 %gather_fusion = f32[98048,16]{1,0:T(8,128)} fusion(f32[16,128]{0,1:T(8,128)S(1)} %copy.88, s32[98304]{0:T(1024)S(1)} %pad_clamp_fusion.1), kind=kCustom, calls=%fused_computation | custom fusion | bytes 12942336 | tf_op jit(solution)/shard_map/jit(_take)/gather | solution.py:40
  228.7 27.7 %copy.89 = f32[98048,16]{0,1:T(8,128)} copy(f32[98048,16]{1,0:T(8,128)} %gather_fusion) | data formatting | bytes 12550144 | tf_op jit(solution)/shard_map/jit(_take)/gather | solution.py:40
  256.4 10.9 %reshape.176 = f32[256,383,16]{1,0,2:T(8,128)} reshape(f32[98048,16]{0,1:T(8,128)} %copy.89) | data formatting | bytes 12550144 | tf_op jit(solution)/shard_map/jit(_take)/gather | solution.py:40
  268.0 183.3 %gather_fusion.1 = f32[99330,16]{1,0:T(8,128)} fusion(f32[16,128]{0,1:T(8,128)S(1)} %copy.88, s32[100352]{0:T(1024)S(1)} %pad_clamp_fusion), kind=kCustom, calls=%fused_computation.1 | custom fusion | bytes 13111560 | tf_op jit(solution)/shard_map/jit(_take)/gather | solution.py:40
  451.2 28.0 %copy.96 = f32[99330,16]{0,1:T(8,128)} copy(f32[99330,16]{1,0:T(8,128)} %gather_fusion.1) | data formatting | bytes 12714240 | tf_op jit(solution)/shard_map/jit(_take)/gather | solution.py:40
  479.2 15.5 %reshape.184 = f32[258,385,16]{1,0,2:T(8,128)} reshape(f32[99330,16]{0,1:T(8,128)} %copy.96) | data formatting | bytes 12714240 | tf_op jit(solution)/shard_map/jit(_take)/gather | solution.py:40
  494.9 3.1 fusion.5
  498.0 9.4 convolution_convert_fusion.1
  508.1 3.1 collective-permute-start
  511.3 2.9 collective-permute-done
  515.4 6.4 fusion.9
  522.6 1.3 collective-permute-start.1
  524.5 5.1 collective-permute-done.1
  530.2 8.0 fusion.1
  539.1 14.5 %fusion = bf16[256,8192]{1,0:T(8,128)(2,1)} fusion(bf16[256,3,256]{0,2,1:T(8,128)(2,1)S(1)} %add_convert_fusion, bf16[8192,3,256]{2,0,1:T(8,128)(2,1)} %param.8), kind=kOutput, calls=%fused_computation.7 | convolution fusion | flops 3223322624 | bytes 17170432 | tf_op jit(solution)/shard_map/dot_general | solution.py:113
  553.6 10.4 convolution_convert_fusion
  564.8 320.6 %all-gather.7.cloned.1.call-done = bf16[4096,8192]{1,0:T(8,128)(2,1)} async-done(((bf16[256,8192]{1,0:T(8,128)(2,1)}), bf16[4096,8192]{1,0:T(8,128)(2,1)}) %all-gather.7.cloned.1.call-update) | async-done | bytes 67108880 | tf_op jit(solution)/shard_map/all_gather | solution.py:121
  885.4 25.0 %reduce_sum.31 = bf16[256,8192]{1,0:T(8,128)(2,1)} reduce(bf16[16,256,8192]{2,1,0:T(8,128)(2,1)} %bitcast.29, bf16[]{:T(256)} %constant.30.clone.1), dimensions={0}, to_apply=%region_1.2 | reduce | flops 31457280 | bytes 71303168 | tf_op jit(solution)/shard_map/reduce_sum | solution.py:120
  910.4 3.3 convert_element_type.150
  913.9 1.3 copy-done.1
  915.2 1.7 fusion.8
  917.7 123.6 %reduce-scatter.2.cloned.1.call-done = bf16[1024,3,256]{2,0,1:T(8,128)(2,1)} async-done(((bf16[8192,3,256]{2,0,1:T(8,128)(2,1)}), bf16[1024,3,256]{2,0,1:T(8,128)(2,1)}) %reduce-scatter.2.cloned.1.call-update) | async-done | bytes 1572880 | tf_op jit(solution)/shard_map/reduce_scatter | solution.py:134
  (75 shorter events, 9.9 us)
Async XLA Ops:
  7.2 487.7 %all-gather.5.cloned.1.call-start = ((), (), s32[]{:S(2)}) async-start(), calls=%async_computation.1 | async-start | bytes 4456448 | tf_op jit(solution)/shard_map/all_gather | solution.py:53
  7.9 877.5 %all-gather.7.cloned.1.call-start = ((), (), s32[]{:S(2)}) async-start(), calls=%async_computation.3 | async-start | bytes 71303168 | tf_op jit(solution)/shard_map/all_gather | solution.py:121
  9.0 16.7 %copy-start.5 = (bf16[512]{0:T(512)(128)(2,1)S(1)}, bf16[512]{0:T(512)(128)(2,1)}, u32[]{:S(2)}) copy-start(bf16[512]{0:T(512)(128)(2,1)} %param.7) | copy-start | bytes 3076
  9.0 38.7 %copy-start.4 = (f32[16,128]{1,0:T(8,128)S(1)}, f32[16,128]{1,0:T(8,128)}, u32[]{:S(2)}) copy-start(f32[16,128]{1,0:T(8,128)} %param.10) | copy-start | bytes 24580
  479.2 15.6 %copy-start.3 = (f32[3,3,256]{2,1,0:T(4,128)S(1)}, f32[3,3,256]{2,1,0:T(4,128)}, u32[]{:S(2)}) copy-start(f32[3,3,256]{2,1,0:T(4,128)} %param.9) | copy-start | bytes 27652
  508.1 6.0 collective-permute-start
  522.6 7.0 collective-permute-start.1
  553.5 487.8 %reduce-scatter.2.cloned.1.call-start = ((), (), s32[]{:S(2)}) async-start(), calls=%async_computation.2 | async-start | bytes 14155776 | tf_op jit(solution)/shard_map/reduce_scatter | solution.py:134
  910.4 3.5 copy-start
  910.4 4.8 copy-start.1
  910.4 6.5 copy-start.2
Sparse Core Ops, SparseCore 0:
  9.7 41.0 all-gather.4
  553.7 331.6 all-gather.6
  889.9 151.3 reduce-scatter.1
